TPU v7x, 32 devices: a whole 2x2x4 slice. The times are simulated.
32 devices in a mesh: dp: 16 (over z, y, core), tensor: 2 (over x).
Axes of the slice: x: 2, y: 2, z: 4, core: 2. Of those that a mesh axis runs over, the one named last changes fastest.
Arguments:
- projected: bfloat16 [3, 8192, 2560], P(None, 'dp', 'tensor'), may hold values from -40 to 40
- residue_counts: int32 [16], P('dp'), may hold values from 64 to 512, as said below
- migrate_plan: int32 [16], P('dp'), may hold values from 0 to 1, as said below
- out_weight: bfloat16 [2560, 2560], P('tensor', 'dp'), may hold values from -0.125 to 0.125
- out_cotangent: bfloat16 [32, 512, 2560], P('dp', None, 'tensor'), may hold values from -6 to 6
Outputs:
- layer_out: bfloat16 [32, 512, 2560], P('dp', None, 'tensor')
- grad_projected: bfloat16 [3, 8192, 2560], P(None, 'dp', 'tensor')
- grad_weight: float32 [2560, 2560], P('tensor', 'dp')
Inputs may be any that keep to these rules, and one draw needn't show every extreme that they name: `residue_counts`: some tile has all 512 positions real, and some has exactly 64. migrate_plan[o] = 1 exactly where the sum of residue_counts over the 1 tiles of o exceeds that of its partner (o + 8) % 16 by more than 128, else 0; so never both devices of a pair have 1.
All inputs are finite; a program needn't handle non-finite values.
Results may differ from a plain program's by a relative error of at most 0.02.
Values may be sent and summed in bfloat16 or wider, within the bound.
A program may use at most 128 MiB of HBM per device.

v0:
```python
import jax
import jax.numpy as jnp
from jax import lax
from jax.sharding import PartitionSpec as P

HEAD_DIM = 64


def shifted(shard, axis, by):
    peers = lax.axis_size(axis)
    return lax.ppermute(shard, axis, [(i, (i + by) % peers) for i in range(peers)])


def attend(tile_qkv, count):
    length = tile_qkv.shape[1]
    columns = tile_qkv.shape[2]
    head_count = columns // HEAD_DIM
    queries = tile_qkv[0].reshape(length, head_count, HEAD_DIM)
    key_rows = tile_qkv[1].reshape(length, head_count, HEAD_DIM)
    values = tile_qkv[2].reshape(length, head_count, HEAD_DIM)
    scores = jnp.einsum(
        "qhd,khd->hqk", queries, key_rows, preferred_element_type=jnp.float32
    ) * HEAD_DIM ** (-0.5)
    position = lax.iota(jnp.int32, length)
    live_mask = position < count
    scores = jnp.where(live_mask[None, None, :], scores, -1000000000.0)
    row_max = jnp.max(scores, axis=2, keepdims=True)
    exponent = jnp.exp(scores - row_max)
    weights = (exponent / jnp.sum(exponent, axis=2, keepdims=True)).astype(jnp.bfloat16)
    context = jnp.einsum("hqk,khd->qhd", weights, values, preferred_element_type=jnp.float32)
    context = context * live_mask.astype(jnp.float32)[:, None, None]
    return context.reshape(length, columns)


def tile_grad(tile_qkv, count, tile_cot):
    _, pullback = jax.vjp(lambda operand: attend(operand, count), tile_qkv)
    return pullback(tile_cot.astype(jnp.float32))[0]


def shards(projected, residue_counts, migrate_plan, out_weight, out_cotangent):
    home_tiles = residue_counts.shape[0]
    length = projected.shape[1] // home_tiles
    columns = projected.shape[2]
    half_axis = lax.axis_size("dp") // 2
    home_qkv = projected.reshape(3, home_tiles, length, columns)
    sent_flag = migrate_plan[0]
    guest_meta = jnp.stack([residue_counts[home_tiles - 1] * sent_flag, sent_flag])
    guest_tile, guest_info = shifted((home_qkv[:, home_tiles - 1], guest_meta), "dp", half_axis)
    slot_qkv = jnp.concatenate([home_qkv, guest_tile[:, None]], axis=1)
    keep_last = residue_counts[home_tiles - 1] * (1 - sent_flag)
    live_counts = jnp.concatenate(
        [residue_counts[: home_tiles - 1], keep_last[None], guest_info[0:1]]
    ).astype(jnp.int32)
    context = jax.vmap(attend, in_axes=(1, 0))(slot_qkv, live_counts).astype(jnp.bfloat16)
    row_count = context.shape[0] * length
    flat_ctx = context.reshape(row_count, columns)
    whole_weight = lax.all_gather(out_weight, "dp", axis=1, tiled=True)
    partial_value = jnp.dot(flat_ctx, whole_weight, preferred_element_type=jnp.float32)
    summed = lax.psum_scatter(
        partial_value.astype(jnp.bfloat16), "tensor", scatter_dimension=1, tiled=True
    )
    layer_out = summed.reshape(home_tiles + 1, length, -1)
    full_cot = lax.all_gather(out_cotangent, "tensor", axis=2, tiled=True).reshape(row_count, -1)
    contract_cols = (((1,), (1,)), ((), ()))
    grad_context = lax.dot_general(
        full_cot, whole_weight, contract_cols, preferred_element_type=jnp.float32
    )
    grad_context = grad_context.astype(jnp.bfloat16).reshape(home_tiles + 1, length, columns)
    weight_term = lax.dot_general(
        flat_ctx, full_cot, (((0,), (0,)), ((), ())), preferred_element_type=jnp.float32
    )
    grad_weight = lax.psum_scatter(
        weight_term.astype(jnp.bfloat16), "dp", scatter_dimension=1, tiled=True
    ).astype(jnp.float32)
    context_back = shifted(grad_context[home_tiles], "dp", half_axis)
    last_cot = jnp.where(sent_flag > 0, context_back, grad_context[home_tiles - 1])
    home_cot = jnp.concatenate([grad_context[: home_tiles - 1], last_cot[None]], axis=0)
    home_grads = jax.vmap(tile_grad, in_axes=(1, 0, 0), out_axes=1)(
        home_qkv, residue_counts, home_cot
    )
    grad_projected = home_grads.reshape(3, home_tiles * length, columns)
    return (layer_out, grad_projected, grad_weight)


def solution(mesh):
    in_specs = (
        P(None, "dp", "tensor"),
        P("dp"),
        P("dp"),
        P("tensor", "dp"),
        P("dp", None, "tensor"),
    )
    out_specs = (P("dp", None, "tensor"), P(None, "dp", "tensor"), P("tensor", "dp"))
    return jax.shard_map(shards, mesh=mesh, in_specs=in_specs, out_specs=out_specs, check_vma=False)
```

profile of v0, /device:TPU:0, one launch (start us, length us, event | category | flops | bytes accessed | tf_op | source)
XLA Modules:
  0.0 527.2 jit_solution(4431982934832433540)
XLA Ops:
  7.2 0.0 all-gather.5.cloned.1.call-start
  7.2 4.4 copy.29
  11.7 0.0 all-gather.3.cloned.1.call-start
  11.7 4.1 collective-permute-start
  17.1 0.1 pad_add_fusion
  17.2 0.0 collective-permute-start.1
  17.2 0.0 all-gather.3.cloned.1.call-update
  17.3 0.0 reduce-scatter.5.cloned.1.call-start
  17.3 207.8 %collective-permute-done.1 = s32[2]{0:T(128)S(1)} collective-permute-done((s32[2]{0:T(128)S(1)}, s32[2]{0:T(128)S(1)}, u32[]{:S(2)}, u32[]{:S(2)}) %collective-permute-start.1) | collective-permute-done | bytes 40 | tf_op jit(solution)/shard_map/ppermute | solution.py:11
  225.1 0.1 pad_add_fusion.1
  225.2 0.1 iota_compare_fusion
  225.3 5.1 pad_maximum_fusion
  230.3 4.4 copy.24
  234.8 4.4 copy.25
  239.2 2.6 copy.26
  241.8 22.2 %fusion.52 = (f32[2,20,512]{2,1,0:T(8,128)S(1)}, f32[2,20,512,512]{2,3,1,0:T(8,128)}) fusion(pred[2,512]{1,0:T(4,128)(4,1)S(1)} %get-tuple-element.14, bf16[2,512,20,64]{1,3,2,0:T(8,128)(2,1)} %bitcast.89, bf16[2,512,20,64]{1,3,2,0:T(8,128)(2,1)} %bitcast.90), kind=kOutput, calls=%fused_computation.75 | convolution fusion | flops 1384120832 | bytes 47268864 | tf_op jit(solution)/shard_map/vmap()/sub | solution.py:28
  263.9 15.7 %multiply_convert_fusion = bf16[2,20,64,512]{3,2,1,0:T(8,128)(2,1)S(1)} fusion(f32[2,512]{1,0:T(2,128)S(1)} %get-tuple-element.15, bf16[2,512,20,64]{1,3,2,0:T(8,128)(2,1)} %bitcast.87, f32[2,20,512,512]{2,3,1,0:T(8,128)} %get-tuple-element.17, f32[2,20,512]{2,1,0:T(8,128)S(1)} %get-tuple-element.16), kind=kOutput, calls=%fused_computation.41 | convolution fusion | flops 1365770240 | bytes 47271936 | tf_op jit(solution)/shard_map/vmap(hqk,khd->qhd)/dot_general | solution.py:30
  279.7 0.0 all-gather.5.cloned.1.call-done
  279.7 11.6 %bitcast_convert_fusion = bf16[1280,2560]{0,1:T(8,128)(2,1)} fusion(bf16[2,512,1280]{1,2,0:T(8,128)(2,1)S(1)} %bitcast.83, bf16[2,512,2560]{1,2,0:T(8,128)(2,1)} %all-gather.5.cloned.1.call-done), kind=kOutput, calls=%fused_computation.24 | convolution fusion | flops 6714163200 | bytes 14417920 | tf_op jit(solution)/shard_map/dot_general | solution.py:69
  291.3 0.0 reduce-scatter.5.cloned.1.call-update
  291.3 0.4 reduce-scatter.3.cloned.1.call-start
  291.7 3.8 fusion.51
  295.5 0.6 copy.33
  296.2 2.1 copy.32
  298.3 3.0 copy.36
  301.3 4.8 fusion.11
  306.1 5.1 fusion.47
  311.2 3.9 copy-done
  315.1 2.7 copy.28
  317.9 0.7 copy.47
  318.6 8.0 %copy.30 = bf16[2,512,2560]{2,1,0:T(8,128)(2,1)} copy(bf16[2,512,2560]{1,2,0:T(8,128)(2,1)} %all-gather.5.cloned.1.call-done) | data formatting | bytes 10485760 | tf_op jit(solution)/shard_map/all_gather | solution.py:63
  326.6 10.9 %convolution_convert_fusion.2 = bf16[1024,1280]{1,0:T(8,128)(2,1)S(1)} fusion(bf16[1024,2560]{1,0:T(8,128)(2,1)} %bitcast.82, bf16[1280,2560]{0,1:T(8,128)(2,1)} %all-gather.3.cloned.1.call-done), kind=kOutput, calls=%fused_computation.43 | convolution fusion | flops 6712197120 | bytes 14417920 | tf_op jit(solution)/shard_map/dot_general | solution.py:65
  337.5 1.5 copy-done.7
  339.0 1.1 slice.45
  340.1 8.9 %convolution_convert_fusion.1 = bf16[1024,2560]{1,0:T(8,128)(2,1)} fusion(bf16[1024,1280]{0,1:T(8,128)(2,1)S(1)} %bitcast.88, bf16[1280,2560]{0,1:T(8,128)(2,1)S(1)} %copy-done.8), kind=kOutput, calls=%fused_computation.39 | convolution fusion | flops 6713507840 | bytes 14417920 | tf_op jit(solution)/shard_map/dot_general | solution.py:58
  349.0 76.2 %collective-permute-done.2 = bf16[512,1280]{1,0:T(8,128)(2,1)} collective-permute-done((bf16[512,1280]{1,0:T(8,128)(2,1)}, bf16[512,1280]{1,0:T(8,128)(2,1)}, u32[]{:S(2)}, u32[]{:S(2)}) %collective-permute-start.2) | collective-permute-done | bytes 1310752 | tf_op jit(solution)/shard_map/ppermute | solution.py:11
  425.3 1.9 fusion.36
  427.1 2.1 copy.31
  429.2 23.0 %convert_reduce_fusion = (f32[20,512]{1,0:T(8,128)S(1)}, pred[20,512,512]{1,2,0:T(32,128)(4,1)}, f32[20,512]{1,0:T(8,128)S(1)}, bf16[20,512,512]{1,2,0:T(8,128)(2,1)}) fusion(f32[20,512]{1,0:T(8,128)S(1)} %get-tuple-element.18, f32[20,512,512]{1,2,0:T(8,128)} %copy-done, pred[512]{0:T(512)(128)(4,1)S(1)} %get-tuple-element.21, ...), kind=kOutput, calls=%fused_computation.12 | convolution fusion | flops 729395200 | bytes 40798720 | tf_op jit(solution)/shard_map/vmap(transpose(jvp(hqk,khd->qhd)))/dot_general | solution.py:30
  452.3 22.0 %fusion.48 = (f32[20,512]{1,0:T(8,128)S(1)}, f32[20,512,512]{1,2,0:T(8,128)}) fusion(f32[20,512]{1,0:T(8,128)S(1)} %get-tuple-element.18, f32[20,512,512]{1,2,0:T(8,128)} %copy-done, pred[512]{0:T(512)(128)(4,1)S(1)} %get-tuple-element.21, f32[20,512]{1,0:T(8,128)S(1)} %neg.10, f32[20,512]{1,0:T(8,128)S(1)} %fusion.47, ...), kind=kLoop, calls=%fused_computation.73 | loop fusion | flops 41932800 | bytes 52593152 | tf_op jit(solution)/shard_map/vmap(transpose(jvp()))/reduce_sum | solution.py:28
  474.4 11.0 %fusion.35 = bf16[20,512,64]{1,2,0:T(8,128)(2,1)} fusion(bf16[512,20,64]{0,2,1:T(8,128)(2,1)S(1)} %bitcast.81, f32[20,512,512]{1,2,0:T(8,128)} %get-tuple-element.4, pred[20,512,512]{1,2,0:T(32,128)(4,1)S(1)} %copy-done.9, f32[20,512]{1,0:T(8,128)S(1)} %negate_divide_fusion, pred[512]{0:T(512)(128)(4,1)S(1)} %get-tuple-element.21), kind=kOutput, calls=%fused_computation.53 | convolution fusion | flops 692715520 | bytes 28877312 | tf_op jit(solution)/shard_map/vmap(transpose(jvp(qhd,khd->hqk)))/dot_general | solution.py:21
  485.4 1.6 copy.40
  487.0 12.9 %fusion.34 = bf16[20,512,64]{1,2,0:T(8,128)(2,1)} fusion(bf16[512,20,64]{0,2,1:T(8,128)(2,1)S(1)} %bitcast.79, f32[20,512,512]{1,2,0:T(8,128)} %get-tuple-element.4, pred[20,512,512]{1,2,0:T(32,128)(4,1)} %get-tuple-element.6, f32[20,512]{1,0:T(8,128)S(1)} %negate_divide_fusion, pred[512]{0:T(512)(128)(4,1)S(1)} %get-tuple-element.21), kind=kOutput, calls=%fused_computation.52 | convolution fusion | flops 692715520 | bytes 28877312 | tf_op jit(solution)/shard_map/vmap(transpose(jvp(qhd,khd->hqk)))/dot_general | solution.py:21
  499.9 1.6 copy.38
  501.5 11.4 %fusion.31 = bf16[20,64,512]{2,1,0:T(8,128)(2,1)} fusion(f32[20,512]{1,0:T(8,128)S(1)} %fusion.47, f32[1,512,20,64]{1,3,2,0:T(8,128)} %bitcast.86, f32[512]{0:T(512)S(1)} %get-tuple-element.22, f32[20,512,512]{1,2,0:T(8,128)} %copy-done, f32[20,512]{1,0:T(8,128)S(1)} %get-tuple-element.18, pred[512]{0:T(512)(128)(4,1)S(1)} %get-tuple-element.21), kind=kOutput, calls=%fused_computation.51 | convolution fusion | flops 698613760 | bytes 24988160 | tf_op jit(solution)/shard_map/vmap(transpose(jvp(hqk,khd->qhd)))/dot_general | solution.py:30
  512.9 2.4 copy.35
  515.3 3.2 add_bitcast_fusion
  518.5 1.9 convert_element_type.113
  (29 shorter events, 0.1 us)
Async XLA Ops:
  7.2 272.5 %all-gather.5.cloned.1.call-start = ((), (), s32[]{:S(2)}) async-start(), calls=%async_computation.4 | async-start | bytes 7864320 | tf_op jit(solution)/shard_map/all_gather | solution.py:63
  11.7 314.9 %all-gather.3.cloned.1.call-start = ((), (), s32[]{:S(2)}) async-start(), calls=%async_computation.2 | async-start | bytes 6963200 | tf_op jit(solution)/shard_map/all_gather | solution.py:57
  11.7 213.6 %collective-permute-start = (bf16[3,512,1280]{2,1,0:T(8,128)(2,1)}, bf16[3,512,1280]{2,1,0:T(8,128)(2,1)}, u32[]{:S(2)}, u32[]{:S(2)}) collective-permute-start(bf16[3,512,1280]{2,1,0:T(8,128)(2,1)} %param.5), channel_id=1, source_target_pairs={{0,16},{2,18},{4,20},{6,22},{8,24},{10,26},{12,28},{14,30},{16,0},... | collective-permute-start | bytes 11796488 | tf_op jit(solution)/shard_map/ppermute | solution.py:11
  17.2 207.9 %collective-permute-start.1 = (s32[2]{0:T(128)S(1)}, s32[2]{0:T(128)S(1)}, u32[]{:S(2)}, u32[]{:S(2)}) collective-permute-start(s32[2]{0:T(128)S(1)} %pad_add_fusion), channel_id=1, source_target_pairs={{0,16},{2,18},{4,20},{6,22},{8,24},{10,26},{12,28},{14,30},{16,0},... | collective-permute-start | bytes 32 | tf_op jit(solution)/shard_map/ppermute | solution.py:11
  17.3 501.2 %reduce-scatter.5.cloned.1.call-start = ((), (), s32[]{:S(2)}) async-start(), calls=%async_computation.5 | async-start | bytes 6963200 | tf_op jit(solution)/shard_map/reduce_scatter | solution.py:72
  279.7 11.6 %copy-start.5 = (bf16[2,20,64,512]{3,2,1,0:T(8,128)(2,1)}, bf16[2,20,64,512]{3,2,1,0:T(8,128)(2,1)S(1)}, u32[]{:S(2)}) copy-start(bf16[2,20,64,512]{3,2,1,0:T(8,128)(2,1)S(1)} %multiply_convert_fusion) | copy-start | bytes 7864324
  291.3 229.1 %reduce-scatter.3.cloned.1.call-start = ((), (), s32[]{:S(2)}) async-start(), calls=%async_computation.3 | async-start | bytes 7864320 | tf_op jit(solution)/shard_map/reduce_scatter | solution.py:59
  296.2 9.9 %copy-start.3 = (bf16[1,512,1280]{1,2,0:T(8,128)(2,1)}, bf16[1,512,1280]{1,2,0:T(8,128)(2,1)S(1)}, u32[]{:S(2)}) copy-start(bf16[1,512,1280]{1,2,0:T(8,128)(2,1)S(1)} %copy.33) | copy-start | bytes 3932164
  298.3 7.8 %copy-start.1 = (bf16[1,512,1280]{1,2,0:T(8,128)(2,1)}, bf16[1,512,1280]{1,2,0:T(8,128)(2,1)S(1)}, u32[]{:S(2)}) copy-start(bf16[1,512,1280]{1,2,0:T(8,128)(2,1)S(1)} %copy.32) | copy-start | bytes 3932164
  306.1 9.0 %copy-start = (f32[20,512,512]{1,2,0:T(8,128)}, f32[20,512,512]{1,2,0:T(8,128)S(1)}, u32[]{:S(2)}) copy-start(f32[20,512,512]{1,2,0:T(8,128)S(1)} %get-tuple-element.19) | copy-start | bytes 62914564
  306.1 9.0 %copy-start.6 = (bf16[2,20,64,512]{3,2,1,0:T(8,128)(2,1)S(1)}, bf16[2,20,64,512]{3,2,1,0:T(8,128)(2,1)}, u32[]{:S(2)}) copy-start(bf16[2,20,64,512]{3,2,1,0:T(8,128)(2,1)} %copy-done.5) | copy-start | bytes 7864324
  326.6 13.5 %copy-start.8 = (bf16[1280,2560]{0,1:T(8,128)(2,1)S(1)}, bf16[1280,2560]{0,1:T(8,128)(2,1)}, u32[]{:S(2)}) copy-start(bf16[1280,2560]{0,1:T(8,128)(2,1)} %all-gather.3.cloned.1.call-done) | copy-start | bytes 19660804
  337.5 1.5 copy-start.7
  340.1 85.1 %collective-permute-start.2 = (bf16[512,1280]{1,0:T(8,128)(2,1)}, bf16[512,1280]{1,0:T(8,128)(2,1)}, u32[]{:S(2)}, u32[]{:S(2)}) collective-permute-start(bf16[512,1280]{1,0:T(8,128)(2,1)} %slice.45), channel_id=1, source_target_pairs={{0,16},{2,18},{4,20},{6,22},{8,24},{10,26},{12,28},{14,30},{16,0},... | collective-permute-start | bytes 3932168 | tf_op jit(solution)/shard_map/ppermute | solution.py:11
  452.3 22.1 %copy-start.4 = (bf16[1,512,1280]{1,2,0:T(8,128)(2,1)S(1)}, bf16[1,512,1280]{1,2,0:T(8,128)(2,1)}, u32[]{:S(2)}) copy-start(bf16[1,512,1280]{1,2,0:T(8,128)(2,1)} %copy-done.3) | copy-start | bytes 3932164
  452.3 22.1 %copy-start.9 = (pred[20,512,512]{1,2,0:T(32,128)(4,1)S(1)}, pred[20,512,512]{1,2,0:T(32,128)(4,1)}, u32[]{:S(2)}) copy-start(pred[20,512,512]{1,2,0:T(32,128)(4,1)} %get-tuple-element.6) | copy-start | bytes 15728644
  474.3 12.6 %copy-start.2 = (bf16[1,512,1280]{1,2,0:T(8,128)(2,1)S(1)}, bf16[1,512,1280]{1,2,0:T(8,128)(2,1)}, u32[]{:S(2)}) copy-start(bf16[1,512,1280]{1,2,0:T(8,128)(2,1)} %copy-done.1) | copy-start | bytes 3932164
Sparse Core Ops, SparseCore 0:
  11.8 71.2 all-gather.4
  85.4 87.0 all-gather.2
  291.4 126.7 reduce-scatter.4
  421.1 70.5 reduce-scatter.2
where the time goes:
time: 536 us; the launch traced here: 527 us
  waiting for transfers between devices  284 us (53%)
  matrix products  132 us (25%)
  local copies, waits for them, and re-layouts  51.1 us (10%)
  other arithmetic  39.5 us (7%)
  between operations  15.5 us (3%)
    ppermute x3, waiting for transfers between devices, shifted(): lax.ppermute(shard, axis, [(i, (i + by) % peers) for i in range(peers)])  284 us
    dot_general x3, matrix products, attend(): jnp.einsum('hqk,khd->qhd', weights, values, preferred_element_type=jnp.fl...  50.1 us
    dot_general x3, matrix products, attend(): jnp.einsum('qhd,khd->hqk', queries, key_rows, preferred_element_type=jnp....  28.7 us
    sub x1, matrix products, attend(): exponent = jnp.exp(scores - row_max)  22.2 us
    reduce_sum x1, other arithmetic, attend(): exponent = jnp.exp(scores - row_max)  22 us
    dot_general x1, matrix products, shards(): lax.dot_general(flat_ctx, full_cot, (((0,), (0,)), ((), ())), preferred_e...  11.6 us
    slice x3, local copies, waits for them, and re-layouts, attend(): values = tile_qkv[2].reshape(length, head_count, HEAD_DIM)  11.2 us
    dot_general x1, matrix products, shards(): lax.dot_general(full_cot, whole_weight, contract_cols, preferred_element_...  10.9 us
  transfers between devices with their start and end apart: 7, of which 2 were waited for; matrix products, arithmetic and copies ran while one was open for 40% of the time, Pallas kernels for 0%

commit v1 on v0

v1 whole, which is shorter than its diff:
```python
import functools

import jax
import jax.numpy as jnp
from jax import lax
from jax.experimental import pallas as pl
from jax.experimental.pallas import tpu as pltpu
from jax.sharding import PartitionSpec as P

HEAD_DIM = 64
SCALE = HEAD_DIM ** (-0.5)
LOG2E = 1.4426950408889634
NT = (((1,), (1,)), ((), ()))
NN = (((1,), (0,)), ((), ()))
TN = (((0,), (0,)), ((), ()))


def dot(a, b, dims):
    return lax.dot_general(a, b, dims, preferred_element_type=jnp.float32)


def probs_t(k, q, live_keys):
    s = dot(k, q, NT) * (SCALE * LOG2E)
    s = jnp.where(live_keys, s, -1000000000.0)
    e = jnp.exp2(s - jnp.max(s, axis=0, keepdims=True))
    return e * (1.0 / jnp.sum(e, axis=0, keepdims=True))


def fwd_kernel(count_ref, qkv_ref, ctx_ref):
    length, width = ctx_ref.shape
    live = lax.broadcasted_iota(jnp.int32, (length, 1), 0) < count_ref[0]
    parts = []
    for h in range(width // HEAD_DIM):
        cols = slice(h * HEAD_DIM, (h + 1) * HEAD_DIM)
        p = probs_t(qkv_ref[1, :, cols], qkv_ref[0, :, cols], live).astype(jnp.bfloat16)
        parts.append(dot(p, qkv_ref[2, :, cols], TN))
    ctx = jnp.concatenate(parts, axis=1)
    ctx_ref[...] = jnp.where(live, ctx, 0.0).astype(jnp.bfloat16)


def bwd_kernel(count_ref, qkv_ref, cot_ref, out_ref):
    length, width = cot_ref.shape
    live = lax.broadcasted_iota(jnp.int32, (length, 1), 0) < count_ref[0]
    grads = ([], [], [])
    for h in range(width // HEAD_DIM):
        cols = slice(h * HEAD_DIM, (h + 1) * HEAD_DIM)
        q, k, v = qkv_ref[0, :, cols], qkv_ref[1, :, cols], qkv_ref[2, :, cols]
        cot = jnp.where(live, cot_ref[:, cols], jnp.bfloat16(0))
        p = probs_t(k, q, live)
        dp = dot(v, cot, NT).astype(jnp.bfloat16).astype(jnp.float32)
        t = p * dp
        ds = (t - p * jnp.sum(t, axis=0, keepdims=True)).astype(jnp.bfloat16)
        grads[0].append(dot(ds, k, TN) * SCALE)
        grads[1].append(dot(ds, q, NN) * SCALE)
        grads[2].append(dot(p.astype(jnp.bfloat16), cot, NN))
    for i in range(3):
        out_ref[i] = jnp.concatenate(grads[i], axis=1).astype(jnp.bfloat16)


def block_width(columns):
    return 128 if columns % 128 == 0 else columns


def attend(qkv, count):
    _, length, columns = qkv.shape
    bw = block_width(columns)
    return pl.pallas_call(
        fwd_kernel,
        grid=(columns // bw,),
        in_specs=[
            pl.BlockSpec(memory_space=pltpu.SMEM),
            pl.BlockSpec((3, length, bw), lambda i: (0, 0, i)),
        ],
        out_specs=pl.BlockSpec((length, bw), lambda i: (0, i)),
        out_shape=jax.ShapeDtypeStruct((length, columns), jnp.bfloat16),
        compiler_params=pltpu.CompilerParams(vmem_limit_bytes=32 << 20),
        cost_estimate=pl.CostEstimate(
            flops=20 * length * length * columns, bytes_accessed=8 * length * columns, transcendentals=0
        ),
        name="attend",
    )(count, qkv)


def attend_back(qkv, count, cot):
    _, length, columns = qkv.shape
    bw = block_width(columns)
    return pl.pallas_call(
        bwd_kernel,
        grid=(columns // bw,),
        in_specs=[
            pl.BlockSpec(memory_space=pltpu.SMEM),
            pl.BlockSpec((3, length, bw), lambda i: (0, 0, i)),
            pl.BlockSpec((length, bw), lambda i: (0, i)),
        ],
        out_specs=pl.BlockSpec((3, length, bw), lambda i: (0, 0, i)),
        out_shape=jax.ShapeDtypeStruct((3, length, columns), jnp.bfloat16),
        compiler_params=pltpu.CompilerParams(vmem_limit_bytes=32 << 20),
        cost_estimate=pl.CostEstimate(
            flops=60 * length * length * columns, bytes_accessed=14 * length * columns, transcendentals=0
        ),
        name="attend_back",
    )(count, qkv, cot)


def swapped(shard):
    peers = lax.axis_size("dp")
    half = peers // 2
    return lax.ppermute(shard, "dp", [(i, (i + half) % peers) for i in range(peers)])


def shards(projected, residue_counts, migrate_plan, out_weight, out_cotangent):
    sent = migrate_plan[0] > 0
    far_cot = swapped(out_cotangent[1])
    whole_weight = lax.all_gather(out_weight, "dp", axis=1, tiled=True)
    ctx = attend(projected, residue_counts)
    cot = jnp.where(sent, far_cot, out_cotangent[0])
    full_cot = lax.all_gather(cot, "tensor", axis=1, tiled=True)
    partial_value = dot(ctx, whole_weight, NN).astype(jnp.bfloat16)
    own = lax.psum_scatter(partial_value, "tensor", scatter_dimension=1, tiled=True)
    nothing = jnp.zeros_like(own)
    guest = swapped(jnp.where(sent, own, nothing))
    weight_term = dot(ctx, full_cot, TN).astype(jnp.bfloat16)
    grad_weight = lax.psum_scatter(weight_term, "dp", scatter_dimension=1, tiled=True)
    grad_context = dot(full_cot, whole_weight, NT).astype(jnp.bfloat16)
    grad_projected = attend_back(projected, residue_counts, grad_context)
    layer_out = jnp.stack([jnp.where(sent, nothing, own), guest])
    return (layer_out, grad_projected, grad_weight.astype(jnp.float32))


def solution(mesh):
    in_specs = (
        P(None, "dp", "tensor"),
        P("dp"),
        P("dp"),
        P("tensor", "dp"),
        P("dp", None, "tensor"),
    )
    out_specs = (P("dp", None, "tensor"), P(None, "dp", "tensor"), P("tensor", "dp"))
    return jax.shard_map(shards, mesh=mesh, in_specs=in_specs, out_specs=out_specs, check_vma=False)
```

time: 536 us -> 309 us (0.58); the launches traced: 527 us -> 309 us
  matrix products: 132 us -> 23.7 us
  waiting for transfers between devices: 284 us -> 210 us
  local copies, waits for them, and re-layouts: 51.1 us -> 3.52 us
  Pallas kernels: 0 us -> 41.3 us
  other arithmetic: 39.5 us -> 8.91 us
    ppermute x3 -> x2, waiting for transfers between devices: 284 us -> 94.9 us  [swapped(): lax.ppermute(shard, 'dp', [(i, (i + half) % peers) for i in range(peers)])]
    reduce_scatter x2, waiting for transfers between devices: 0.01 us -> 95.5 us  [the longest x1 71.1 us: shards(): lax.psum_scatter(weight_term, 'dp', scatter_dimension=1, tiled=True)]
    dot_general x9 -> x3, matrix products: 110 us -> 23.7 us  [dot(): return lax.dot_general(a, b, dims, preferred_element_type=jnp.float32)]
    pallas_call x0 -> x2, Pallas kernels: none -> 41.3 us  [the longest x1 26.9 us: attend_back(): pl.pallas_call(bwd_kernel, grid=(columns // bw,), in_specs=[pl.BlockSpec(...]
    reduce_sum x2 -> x0, other arithmetic: 27.1 us -> none  [the longest x1 22 us: attend(): exponent = jnp.exp(scores - row_max)]
    sub x1 -> x0, matrix products: 22.2 us -> none  [attend(): exponent = jnp.exp(scores - row_max)]
    slice x8 -> x0, local copies, waits for them, and re-layouts: 22.1 us -> none  [the longest x3 11.2 us: attend(): values = tile_qkv[2].reshape(length, head_count, HEAD_DIM)]
    all_gather x1, waiting for transfers between devices: 0.02 us -> 18.5 us  [shards(): full_cot = lax.all_gather(cot, 'tensor', axis=1, tiled=True)]
  transfers between devices with their start and end apart: 7 -> 6, of which waited for: 2 -> 4; matrix products, arithmetic and copies ran while one was open for 40% -> 10% of each run, Pallas kernels for 0% -> 13%
where the time goes in v1:
time: 309 us
  waiting for transfers between devices  210 us (68%)
  Pallas kernels  41.3 us (13%)
  matrix products  23.7 us (8%)
  between operations  15.1 us (5%)
  other arithmetic  8.91 us (3%)
  starting transfers between devices  6.68 us (2%)
  local copies, waits for them, and re-layouts  3.52 us (1%)
    ppermute x2, waiting for transfers between devices, swapped(): lax.ppermute(shard, 'dp', [(i, (i + half) % peers) for i in range(peers)])  94.9 us
    reduce_scatter x1, waiting for transfers between devices, shards(): lax.psum_scatter(weight_term, 'dp', scatter_dimension=1, tiled=True)  71.1 us
    pallas_call x1, Pallas kernels, attend_back(): pl.pallas_call(bwd_kernel, grid=(columns // bw,), in_specs=[pl.BlockSpec(...  26.9 us
    reduce_scatter x1, waiting for transfers between devices, shards(): lax.psum_scatter(partial_value, 'tensor', scatter_dimension=1, tiled=True)  24.4 us
    dot_general x3, matrix products, dot(): return lax.dot_general(a, b, dims, preferred_element_type=jnp.float32)  23.7 us
    all_gather x1, waiting for transfers between devices, shards(): full_cot = lax.all_gather(cot, 'tensor', axis=1, tiled=True)  18.5 us
    pallas_call x1, Pallas kernels, attend(): pl.pallas_call(fwd_kernel, grid=(columns // bw,), in_specs=[pl.BlockSpec(...  14.5 us
    ppermute x2, starting transfers between devices, swapped(): lax.ppermute(shard, 'dp', [(i, (i + half) % peers) for i in range(peers)])  6.52 us
  transfers between devices with their start and end apart: 6, of which 4 were waited for; matrix products, arithmetic and copies ran while one was open for 10% of the time, Pallas kernels for 13%

profile of v1, /device:TPU:0, one launch (start us, length us, event | category | flops | bytes accessed | tf_op | source)
XLA Modules:
  0.0 309.0 jit_solution(14803744913075724903)
XLA Ops:
  7.2 0.0 copy-start.2
  7.2 0.0 all-gather.3.cloned.1.call-start
  7.2 0.7 all-gather.3.cloned.1.call-update
  7.9 0.0 all-gather.5.cloned.1.call-start
  8.0 1.4 slice_bitcast_fusion
  9.4 4.1 %collective-permute-start.1 = (bf16[512,1280]{1,0:T(8,128)(2,1)S(1)}, bf16[512,1280]{1,0:T(8,128)(2,1)S(1)}, u32[]{:S(2)}, u32[]{:S(2)}) collective-permute-start(bf16[512,1280]{1,0:T(8,128)(2,1)S(1)} %slice_bitcast_fusion), channel_id=1, source_target_pairs={{0,16},{2,18},{4,20},{6,22},{8,24},{10,26},{12,28},{14,30},{16,0},... | collective-permute-start | bytes 3932168 | tf_op jit(solution)/shard_map/ppermute | solution.py:108
  14.1 94.9 %collective-permute-done.1 = bf16[512,1280]{1,0:T(8,128)(2,1)S(1)} collective-permute-done((bf16[512,1280]{1,0:T(8,128)(2,1)S(1)}, bf16[512,1280]{1,0:T(8,128)(2,1)S(1)}, u32[]{:S(2)}, u32[]{:S(2)}) %collective-permute-start.1) | collective-permute-done | bytes 1310752 | tf_op jit(solution)/shard_map/ppermute | solution.py:108
  109.0 0.0 copy-done.2
  109.0 1.2 bitcast_select_fusion
  110.2 0.0 all-gather.5.cloned.1.call-update
  110.3 0.0 reduce-scatter.3.cloned.1.call-start
  111.0 0.0 copy-start
  111.0 2.1 copy-done
  113.1 14.5 %attend.1 = bf16[512,1280]{1,0:T(8,128)(2,1)S(1)} custom-call(s32[1]{0:T(128)S(6)} %copy.8.count_ref, bf16[3,512,1280]{2,1,0:T(8,128)(2,1)S(1)} %copy-done), custom_call_target="tpu_custom_call" | custom-call | flops 6710886400 | bytes 5242880 | tf_op jit(solution)/shard_map/attend/pallas_call | solution.py:67
  127.5 0.0 all-gather.3.cloned.1.call-done
  127.6 7.7 %convolution_convert_fusion.1 = bf16[512,2560]{1,0:T(8,128)(2,1)} fusion(bf16[512,1280]{1,0:T(8,128)(2,1)S(1)} %attend.1, bf16[1280,2560]{0,1:T(8,128)(2,1)} %all-gather.3.cloned.1.call-done), kind=kOutput, calls=%fused_computation.1 | convolution fusion | flops 3356753920 | bytes 10485760 | tf_op jit(solution)/shard_map/dot_general | solution.py:19
  135.3 0.0 reduce-scatter.3.cloned.1.call-update
  135.3 0.0 reduce-scatter.5.cloned.1.call-start
  135.4 18.5 %all-gather.5.cloned.1.call-done = bf16[512,2560]{1,0:T(8,128)(2,1)} async-done(((bf16[512,1280]{1,0:T(8,128)(2,1)}), bf16[512,2560]{1,0:T(8,128)(2,1)}) %all-gather.5.cloned.1.call-update) | async-done | bytes 2621456 | tf_op jit(solution)/shard_map/all_gather | solution.py:117
  153.9 8.0 %convolution_convert_fusion = bf16[1280,2560]{0,1:T(8,128)(2,1)} fusion(bf16[512,1280]{1,0:T(8,128)(2,1)S(1)} %attend.1, bf16[512,2560]{1,0:T(8,128)(2,1)} %all-gather.5.cloned.1.call-done), kind=kOutput, calls=%fused_computation | convolution fusion | flops 3358720000 | bytes 10485760 | tf_op jit(solution)/shard_map/dot_general | solution.py:19
  161.9 0.0 reduce-scatter.5.cloned.1.call-update
  162.0 7.9 %convolution_convert_fusion.2.cot_ref = bf16[512,1280]{1,0:T(8,128)(2,1)S(1)} fusion(bf16[512,2560]{1,0:T(8,128)(2,1)} %all-gather.5.cloned.1.call-done, bf16[1280,2560]{0,1:T(8,128)(2,1)} %all-gather.3.cloned.1.call-done), kind=kOutput, calls=%fused_computation.2 | convolution fusion | flops 3356098560 | bytes 10485760 | tf_op jit(solution)/shard_map/dot_general | solution.py:19
  169.9 24.4 %reduce-scatter.3.cloned.1.call-done = bf16[512,1280]{1,0:T(8,128)(2,1)} async-done(((bf16[512,2560]{1,0:T(8,128)(2,1)}), bf16[512,1280]{1,0:T(8,128)(2,1)}) %reduce-scatter.3.cloned.1.call-update) | async-done | bytes 1310736 | tf_op jit(solution)/shard_map/reduce_scatter | solution.py:119
  194.3 0.0 copy-start.1
  194.4 2.7 select_bitcast_fusion
  197.0 2.4 collective-permute-start
  199.5 0.0 copy-done.1
  199.5 26.9 %attend_back.1 = bf16[3,512,1280]{2,1,0:T(8,128)(2,1)} custom-call(s32[1]{0:T(128)S(6)} %copy.8.count_ref, bf16[3,512,1280]{2,1,0:T(8,128)(2,1)S(1)} %copy-done.1, bf16[512,1280]{1,0:T(8,128)(2,1)S(1)} %convolution_convert_fusion.2.cot_ref), custom_call_target="tpu_custom_call" | custom-call | flops 20132659200 | bytes 9175040 | tf_op jit(solution)/shard_map/attend_back/pallas_call | solution.py:87
  226.3 71.1 %reduce-scatter.5.cloned.1.call-done = bf16[1280,160]{0,1:T(8,128)(2,1)} async-done(((bf16[1280,2560]{0,1:T(8,128)(2,1)}), bf16[1280,160]{0,1:T(8,128)(2,1)}) %reduce-scatter.5.cloned.1.call-update) | async-done | bytes 409616 | tf_op jit(solution)/shard_map/reduce_scatter | solution.py:123
  297.4 1.9 convert_element_type.15
  299.4 0.0 collective-permute-done
  299.4 3.0 pad_maximum_fusion
Async XLA Ops:
  7.2 101.8 %copy-start.2 = (bf16[2,512,1280]{2,1,0:T(8,128)(2,1)S(1)}, bf16[2,512,1280]{2,1,0:T(8,128)(2,1)}, u32[]{:S(2)}) copy-start(bf16[2,512,1280]{2,1,0:T(8,128)(2,1)} %param.9) | copy-start | bytes 7864324
  7.2 120.4 %all-gather.3.cloned.1.call-start = ((), (), s32[]{:S(2)}) async-start(), calls=%async_computation.2 | async-start | bytes 6963200 | tf_op jit(solution)/shard_map/all_gather | solution.py:114
  7.9 146.0 %all-gather.5.cloned.1.call-start = ((), (), s32[]{:S(2)}) async-start(), calls=%async_computation.4 | async-start | bytes 3932160 | tf_op jit(solution)/shard_map/all_gather | solution.py:117
  9.4 99.6 %collective-permute-start.1 = (bf16[512,1280]{1,0:T(8,128)(2,1)S(1)}, bf16[512,1280]{1,0:T(8,128)(2,1)S(1)}, u32[]{:S(2)}, u32[]{:S(2)}) collective-permute-start(bf16[512,1280]{1,0:T(8,128)(2,1)S(1)} %slice_bitcast_fusion), channel_id=1, source_target_pairs={{0,16},{2,18},{4,20},{6,22},{8,24},{10,26},{12,28},{14,30},{16,0},... | collective-permute-start | bytes 3932168 | tf_op jit(solution)/shard_map/ppermute | solution.py:108
  110.3 84.1 %reduce-scatter.3.cloned.1.call-start = ((), (), s32[]{:S(2)}) async-start(), calls=%async_computation.3 | async-start | bytes 3932160 | tf_op jit(solution)/shard_map/reduce_scatter | solution.py:119
  111.0 2.1 copy-start
  135.3 162.1 %reduce-scatter.5.cloned.1.call-start = ((), (), s32[]{:S(2)}) async-start(), calls=%async_computation.5 | async-start | bytes 6963200 | tf_op jit(solution)/shard_map/reduce_scatter | solution.py:123
  194.3 5.1 %copy-start.1 = (bf16[3,512,1280]{2,1,0:T(8,128)(2,1)S(1)}, bf16[3,512,1280]{2,1,0:T(8,128)(2,1)}, u32[]{:S(2)}) copy-start(bf16[3,512,1280]{2,1,0:T(8,128)(2,1)} %qkv_ref.3) | copy-start | bytes 11796484
  197.0 102.3 %collective-permute-start = (bf16[512,1280]{1,0:T(8,128)(2,1)}, bf16[512,1280]{1,0:T(8,128)(2,1)}, u32[]{:S(2)}, u32[]{:S(2)}) collective-permute-start(bf16[512,1280]{1,0:T(8,128)(2,1)} %get-tuple-element.4), channel_id=1, source_target_pairs={{0,16},{2,18},{4,20},{6,22},{8,24},{10,26},{12,28},{14,30},{16,0},... | collective-permute-start | bytes 3932168 | tf_op jit(solution)/shard_map/ppermute | solution.py:108
Sparse Core Ops, SparseCore 0:
  10.3 101.5 all-gather.2
  114.0 39.8 all-gather.4
  156.7 37.5 reduce-scatter.2
  198.7 98.6 reduce-scatter.4

commit v2 on v1

--- a/solution.py
+++ b/solution.py
@@ -113,6 +113,7 @@
     far_cot = swapped(out_cotangent[1])
     whole_weight = lax.all_gather(out_weight, "dp", axis=1, tiled=True)
     ctx = attend(projected, residue_counts)
+    far_cot, ctx = lax.optimization_barrier((far_cot, ctx))
     cot = jnp.where(sent, far_cot, out_cotangent[0])
     full_cot = lax.all_gather(cot, "tensor", axis=1, tiled=True)
     partial_value = dot(ctx, whole_weight, NN).astype(jnp.bfloat16)

time: 309 us -> 309 us (level)
    ppermute x2, waiting for transfers between devices: 94.9 us -> 77.6 us  [swapped(): lax.ppermute(shard, 'dp', [(i, (i + half) % peers) for i in range(peers)])]
    all_gather x1, waiting for transfers between devices: 18.5 us -> 34.3 us  [shards(): full_cot = lax.all_gather(cot, 'tensor', axis=1, tiled=True)]
  transfers between devices with their start and end apart: 6 -> 6, of which waited for: 4 -> 5; matrix products, arithmetic and copies ran while one was open for 10% -> 10% of each run, Pallas kernels for 13% -> 13%
where the time goes in v2:
time: 309 us
  waiting for transfers between devices  210 us (68%)
  Pallas kernels  41.3 us (13%)
  matrix products  23.7 us (8%)
  between operations  15.1 us (5%)
  other arithmetic  8.88 us (3%)
  starting transfers between devices  6.67 us (2%)
  local copies, waits for them, and re-layouts  3.52 us (1%)
    ppermute x2, waiting for transfers between devices, swapped(): lax.ppermute(shard, 'dp', [(i, (i + half) % peers) for i in range(peers)])  77.6 us
    reduce_scatter x1, waiting for transfers between devices, shards(): lax.psum_scatter(weight_term, 'dp', scatter_dimension=1, tiled=True)  71.1 us
    all_gather x1, waiting for transfers between devices, shards(): full_cot = lax.all_gather(cot, 'tensor', axis=1, tiled=True)  34.3 us
    pallas_call x1, Pallas kernels, attend_back(): pl.pallas_call(bwd_kernel, grid=(columns // bw,), in_specs=[pl.BlockSpec(...  26.9 us
    reduce_scatter x1, waiting for transfers between devices, shards(): lax.psum_scatter(partial_value, 'tensor', scatter_dimension=1, tiled=True)  24.5 us
    dot_general x3, matrix products, dot(): return lax.dot_general(a, b, dims, preferred_element_type=jnp.float32)  23.7 us
    pallas_call x1, Pallas kernels, attend(): pl.pallas_call(fwd_kernel, grid=(columns // bw,), in_specs=[pl.BlockSpec(...  14.5 us
    ppermute x2, starting transfers between devices, swapped(): lax.ppermute(shard, 'dp', [(i, (i + half) % peers) for i in range(peers)])  6.51 us
  transfers between devices with their start and end apart: 6, of which 5 were waited for; matrix products, arithmetic and copies ran while one was open for 10% of the time, Pallas kernels for 13%

profile of v2, /device:TPU:0, one launch (start us, length us, event | category | flops | bytes accessed | tf_op | source)
XLA Modules:
  0.0 308.9 jit_solution(10498195942618176847)
XLA Ops:
  7.2 0.0 all-gather.3.cloned.1.call-start
  7.2 0.7 all-gather.3.cloned.1.call-update
  7.9 0.0 all-gather.5.cloned.1.call-start
  7.9 1.4 slice_bitcast_fusion
  9.4 4.1 %collective-permute-start = (bf16[512,1280]{1,0:T(8,128)(2,1)S(1)}, bf16[512,1280]{1,0:T(8,128)(2,1)S(1)}, u32[]{:S(2)}, u32[]{:S(2)}) collective-permute-start(bf16[512,1280]{1,0:T(8,128)(2,1)S(1)} %slice_bitcast_fusion), channel_id=1, source_target_pairs={{0,16},{2,18},{4,20},{6,22},{8,24},{10,26},{12,28},{14,30},{16,0},... | collective-permute-start | bytes 3932168 | tf_op jit(solution)/shard_map/ppermute | solution.py:108
  14.8 0.0 copy-start
  14.8 2.1 copy-done
  16.9 0.0 copy-start.2
  16.9 14.5 %attend.1 = bf16[512,1280]{1,0:T(8,128)(2,1)S(1)} custom-call(s32[1]{0:T(128)S(6)} %copy.8.count_ref, bf16[3,512,1280]{2,1,0:T(8,128)(2,1)S(1)} %copy-done), custom_call_target="tpu_custom_call" | custom-call | flops 6710886400 | bytes 5242880 | tf_op jit(solution)/shard_map/attend/pallas_call | solution.py:67
  31.3 77.6 %collective-permute-done = bf16[512,1280]{1,0:T(8,128)(2,1)S(1)} collective-permute-done((bf16[512,1280]{1,0:T(8,128)(2,1)S(1)}, bf16[512,1280]{1,0:T(8,128)(2,1)S(1)}, u32[]{:S(2)}, u32[]{:S(2)}) %collective-permute-start) | collective-permute-done | bytes 1310752 | tf_op jit(solution)/shard_map/ppermute | solution.py:108
  109.0 0.0 copy-done.2
  109.0 1.2 bitcast_select_fusion
  110.2 0.0 all-gather.5.cloned.1.call-update
  110.2 0.0 reduce-scatter.3.cloned.1.call-start
  110.3 1.6 all-gather.3.cloned.1.call-done
  111.8 7.7 %convolution_convert_fusion.1 = bf16[512,2560]{1,0:T(8,128)(2,1)} fusion(bf16[512,1280]{1,0:T(8,128)(2,1)S(1)} %attend.1, bf16[1280,2560]{0,1:T(8,128)(2,1)} %all-gather.3.cloned.1.call-done), kind=kOutput, calls=%fused_computation.1 | convolution fusion | flops 3356753920 | bytes 10485760 | tf_op jit(solution)/shard_map/dot_general | solution.py:19
  119.6 0.0 reduce-scatter.3.cloned.1.call-update
  119.6 0.0 reduce-scatter.5.cloned.1.call-start
  119.6 34.3 %all-gather.5.cloned.1.call-done = bf16[512,2560]{1,0:T(8,128)(2,1)} async-done(((bf16[512,1280]{1,0:T(8,128)(2,1)}), bf16[512,2560]{1,0:T(8,128)(2,1)}) %all-gather.5.cloned.1.call-update) | async-done | bytes 2621456 | tf_op jit(solution)/shard_map/all_gather | solution.py:118
  153.9 8.0 %convolution_convert_fusion = bf16[1280,2560]{0,1:T(8,128)(2,1)} fusion(bf16[512,1280]{1,0:T(8,128)(2,1)S(1)} %attend.1, bf16[512,2560]{1,0:T(8,128)(2,1)} %all-gather.5.cloned.1.call-done), kind=kOutput, calls=%fused_computation | convolution fusion | flops 3358720000 | bytes 10485760 | tf_op jit(solution)/shard_map/dot_general | solution.py:19
  161.9 0.0 reduce-scatter.5.cloned.1.call-update
  162.0 7.9 %convolution_convert_fusion.2.cot_ref = bf16[512,1280]{1,0:T(8,128)(2,1)S(1)} fusion(bf16[512,2560]{1,0:T(8,128)(2,1)} %all-gather.5.cloned.1.call-done, bf16[1280,2560]{0,1:T(8,128)(2,1)} %all-gather.3.cloned.1.call-done), kind=kOutput, calls=%fused_computation.2 | convolution fusion | flops 3356098560 | bytes 10485760 | tf_op jit(solution)/shard_map/dot_general | solution.py:19
  169.9 24.5 %reduce-scatter.3.cloned.1.call-done = bf16[512,1280]{1,0:T(8,128)(2,1)} async-done(((bf16[512,2560]{1,0:T(8,128)(2,1)}), bf16[512,1280]{1,0:T(8,128)(2,1)}) %reduce-scatter.3.cloned.1.call-update) | async-done | bytes 1310736 | tf_op jit(solution)/shard_map/reduce_scatter | solution.py:120
  194.3 0.0 copy-start.1
  194.3 2.7 select_bitcast_fusion
  197.0 2.4 collective-permute-start.1
  199.4 0.0 copy-done.1
  199.5 26.9 %attend_back.1 = bf16[3,512,1280]{2,1,0:T(8,128)(2,1)} custom-call(s32[1]{0:T(128)S(6)} %copy.8.count_ref, bf16[3,512,1280]{2,1,0:T(8,128)(2,1)S(1)} %copy-done.1, bf16[512,1280]{1,0:T(8,128)(2,1)S(1)} %convolution_convert_fusion.2.cot_ref), custom_call_target="tpu_custom_call" | custom-call | flops 20132659200 | bytes 9175040 | tf_op jit(solution)/shard_map/attend_back/pallas_call | solution.py:87
  226.3 71.1 %reduce-scatter.5.cloned.1.call-done = bf16[1280,160]{0,1:T(8,128)(2,1)} async-done(((bf16[1280,2560]{0,1:T(8,128)(2,1)}), bf16[1280,160]{0,1:T(8,128)(2,1)}) %reduce-scatter.5.cloned.1.call-update) | async-done | bytes 409616 | tf_op jit(solution)/shard_map/reduce_scatter | solution.py:124
  297.4 1.9 convert_element_type.15
  299.4 0.0 collective-permute-done.1
  299.4 3.0 pad_maximum_fusion
Async XLA Ops:
  7.2 104.7 %all-gather.3.cloned.1.call-start = ((), (), s32[]{:S(2)}) async-start(), calls=%async_computation.2 | async-start | bytes 6963200 | tf_op jit(solution)/shard_map/all_gather | solution.py:114
  7.9 146.0 %all-gather.5.cloned.1.call-start = ((), (), s32[]{:S(2)}) async-start(), calls=%async_computation.4 | async-start | bytes 3932160 | tf_op jit(solution)/shard_map/all_gather | solution.py:118
  9.4 99.6 %collective-permute-start = (bf16[512,1280]{1,0:T(8,128)(2,1)S(1)}, bf16[512,1280]{1,0:T(8,128)(2,1)S(1)}, u32[]{:S(2)}, u32[]{:S(2)}) collective-permute-start(bf16[512,1280]{1,0:T(8,128)(2,1)S(1)} %slice_bitcast_fusion), channel_id=1, source_target_pairs={{0,16},{2,18},{4,20},{6,22},{8,24},{10,26},{12,28},{14,30},{16,0},... | collective-permute-start | bytes 3932168 | tf_op jit(solution)/shard_map/ppermute | solution.py:108
  14.8 2.1 copy-start
  16.9 92.1 %copy-start.2 = (bf16[2,512,1280]{2,1,0:T(8,128)(2,1)S(1)}, bf16[2,512,1280]{2,1,0:T(8,128)(2,1)}, u32[]{:S(2)}) copy-start(bf16[2,512,1280]{2,1,0:T(8,128)(2,1)} %param.9) | copy-start | bytes 7864324
  110.2 84.1 %reduce-scatter.3.cloned.1.call-start = ((), (), s32[]{:S(2)}) async-start(), calls=%async_computation.3 | async-start | bytes 3932160 | tf_op jit(solution)/shard_map/reduce_scatter | solution.py:120
  119.6 177.8 %reduce-scatter.5.cloned.1.call-start = ((), (), s32[]{:S(2)}) async-start(), calls=%async_computation.5 | async-start | bytes 6963200 | tf_op jit(solution)/shard_map/reduce_scatter | solution.py:124
  194.3 5.1 %copy-start.1 = (bf16[3,512,1280]{2,1,0:T(8,128)(2,1)S(1)}, bf16[3,512,1280]{2,1,0:T(8,128)(2,1)}, u32[]{:S(2)}) copy-start(bf16[3,512,1280]{2,1,0:T(8,128)(2,1)} %qkv_ref.3) | copy-start | bytes 11796484
  197.0 102.3 %collective-permute-start.1 = (bf16[512,1280]{1,0:T(8,128)(2,1)}, bf16[512,1280]{1,0:T(8,128)(2,1)}, u32[]{:S(2)}, u32[]{:S(2)}) collective-permute-start(bf16[512,1280]{1,0:T(8,128)(2,1)} %get-tuple-element.8), channel_id=1, source_target_pairs={{0,16},{2,18},{4,20},{6,22},{8,24},{10,26},{12,28},{14,30},{16,0},... | collective-permute-start | bytes 3932168 | tf_op jit(solution)/shard_map/ppermute | solution.py:108
Sparse Core Ops, SparseCore 0:
  10.3 101.5 all-gather.2
  114.0 39.8 all-gather.4
  156.7 37.5 reduce-scatter.2
  198.7 98.6 reduce-scatter.4
